TPU v7x, 128 devices: a whole 4x4x4 slice. The times are simulated.
128 devices in a mesh: row: 8 (over y, x_lo), col: 16 (over x_hi, z, core).
Axes of the slice: x: 4 (x_hi: 2, x_lo: 2; x = x_hi * 2 + x_lo), y: 4, z: 4, core: 2. Of those that a mesh axis runs over, the one named last changes fastest.
Arguments:
- front: float32 [16384, 16384], P('row', 'col'), may hold values from -6 to 6
- contrib: float32 [8192, 16384], P('row', 'col'), may hold values from -6 to 6
- pivot_inverse: float32 [4, 256, 256], replicated, may hold values from -0.0234375 to 0.0234375
- index_map: int32 [2, 32], replicated, may hold values from 0 to 63, as said below
- fill_mask: int32 [64, 64], replicated, may hold values from 0 to 1, as said below
Outputs:
- factored: float32 [16384, 16384], P('row', 'col')
Inputs may be any that keep to these rules, and one draw needn't show every extreme that they name: For each child h, index_map[h, a] = a + t_h(floor(a / 8)), where t_h is nondecreasing, t_h(0) <= 8 and t_h grows by at most 8 from one group to the next. For one of the two children, drawn from the seed, t_h(g) = (g + 1) * 8 for every group g. Hence every parent process row owns exactly 4 of a child's block indices, and the 4 consecutive child block columns held by one device land on distinct parent process columns. 1 marks a block of the fill pattern. It contains every block (index_map[h, a], index_map[h, b]) and is closed under the first 4 steps: for k < 4, i > k, j > k, fill_mask[i, k] = fill_mask[k, j] = 1 implies fill_mask[i, j] = 1.
All inputs are finite; a program needn't handle non-finite values.
Results may differ from a plain program's by a relative error of at most 0.00021.
Values sent between devices are 32-bit elements; how exact they have to be, the bound alone decides.
A program may use at most 192 MiB of HBM per device.

v0:
```python
import jax
import jax.numpy as jnp
from jax import lax
from jax.sharding import PartitionSpec as P

BS = 256
K = 4


exact_mode = lax.Precision.HIGHEST


def from_root(block, axis, holder):
    block = jnp.where(lax.axis_index(axis) == holder, block, jnp.zeros_like(block))
    return lax.psum(block, axis)


def local_rows(block_map, row_index, row_count, child_blocks):
    child_total = block_map.shape[0]
    order_key = block_map % row_count * child_total + jnp.arange(child_total, dtype=jnp.int32)
    ordering = jnp.argsort(order_key)
    mine_rows = lax.dynamic_slice_in_dim(ordering, row_index * child_blocks, child_blocks)
    return block_map[mine_rows] // row_count


def deposit(running, values, row_targets, col_targets, present):
    row_blocks = running.shape[0]
    col_blocks = running.shape[2]
    row_hit = (row_targets[:, :, None] == jnp.arange(row_blocks, dtype=jnp.int32)).astype(
        jnp.float32
    )
    col_hit = (
        (col_targets[:, None] == jnp.arange(col_blocks, dtype=jnp.int32)) & present[:, None]
    ).astype(jnp.float32)
    weight = row_hit[:, :, :, None] * col_hit[None, :, None, :]
    return jnp.einsum("jslc,jxsy->lxcy", weight, values, precision=exact_mode)


def body(front, contrib, pivot_inverse, index_map, fill_mask):
    row_count = lax.axis_size("row")
    col_count = lax.axis_size("col")
    row_index = lax.axis_index("row")
    col_index = lax.axis_index("col")
    row_blocks = front.shape[0] // BS
    col_blocks = front.shape[1] // BS
    child_blocks = contrib.shape[1] // BS
    rows_local = jnp.stack(
        [
            local_rows(index_map[0], row_index, row_count, child_blocks),
            local_rows(index_map[1], row_index, row_count, child_blocks),
        ]
    )
    stripes = contrib.reshape(child_blocks, BS, child_blocks, BS)
    zero_front = jnp.zeros((row_blocks, BS, col_blocks, BS), jnp.float32)
    own_half = col_index // row_count
    own_cols = col_index % row_count * child_blocks + jnp.arange(child_blocks, dtype=jnp.int32)
    targets = index_map[own_half, own_cols]
    matches = (targets % col_count)[None, :] == jnp.arange(col_count, dtype=jnp.int32)[:, None]
    missing = 1 - jnp.any(matches, axis=1).astype(jnp.int32)
    chosen = (
        jnp.sum(jnp.where(matches, jnp.arange(child_blocks, dtype=jnp.int32)[None, :], 0), axis=1)
        + child_blocks * missing
    )
    outgoing = jnp.take(stripes, chosen, axis=2, mode="fill", fill_value=0.0)
    received = lax.all_to_all(outgoing, "col", split_axis=2, concat_axis=2, tiled=True)
    source = jnp.arange(col_count, dtype=jnp.int32)
    src_half = source // row_count
    src_cols = (source % row_count)[:, None] * child_blocks + jnp.arange(
        child_blocks, dtype=jnp.int32
    )[None, :]
    parents = index_map[src_half[:, None], src_cols]
    lands_here = parents % col_count == col_index
    col_targets = jnp.sum(jnp.where(lands_here, parents // col_count, 0), axis=1)
    assembled = deposit(
        zero_front, received, rows_local[src_half].T, col_targets, jnp.any(lands_here, axis=1)
    )
    glob_rows = jnp.arange(row_blocks, dtype=jnp.int32) * row_count + row_index
    glob_cols = jnp.arange(col_blocks, dtype=jnp.int32) * col_count + col_index
    local_mask = fill_mask[glob_rows[:, None], glob_cols[None, :]].astype(jnp.float32)
    blocks = (front.reshape(row_blocks, BS, col_blocks, BS) + assembled) * local_mask[
        :, None, :, None
    ]
    for panel_index in range(K):
        owner_col = panel_index % col_count
        local_col = panel_index // col_count
        owner_row = panel_index % row_count
        local_row = panel_index // row_count
        below_rows = glob_rows > panel_index
        right_cols = glob_cols > panel_index
        column = blocks[:, :, local_col, :]
        inverse = pivot_inverse[panel_index]
        outbound = jnp.where(
            below_rows[:, None, None],
            jnp.einsum("lxz,zy->lxy", column, inverse, precision=exact_mode),
            0.0,
        )
        received_lower = from_root(outbound, "col", owner_col)
        upper_local = jnp.where(right_cols[None, :, None], blocks[local_row], 0.0)
        upper_part = from_root(upper_local, "row", owner_row)
        blocks = blocks - jnp.einsum(
            "lxz,zcy->lxcy", received_lower, upper_part, precision=exact_mode
        )
        replace_rows = (col_index == owner_col) & below_rows
        blocks = blocks.at[:, :, local_col, :].set(
            jnp.where(replace_rows[:, None, None], received_lower, blocks[:, :, local_col, :])
        )
    return blocks.reshape(row_blocks * BS, col_blocks * BS)


def solution(mesh):
    in_specs = (P("row", "col"), P("row", "col"), P(), P(), P())
    out_specs = P("row", "col")
    return jax.shard_map(body, mesh=mesh, in_specs=in_specs, out_specs=out_specs, check_vma=False)
```

profile of v0, /device:TPU:118, one launch (start us, length us, event | category | flops | bytes accessed | tf_op | source)
XLA Modules:
  0.0 1349.0 jit_solution(2061254680718512916)
XLA Ops:
  8.2 5.6 reshape.520
  13.8 4.9 copy.114
  18.6 9.9 gather_fusion.1
  28.5 7.2 select_bitcast_fusion
  35.8 11.6 copy.115
  47.4 6.9 all-to-all-start
  62.1 10.5 reshape.591
  72.9 240.8 %all-to-all-done = f32[4,256,16,256]{3,0,1,2:T(4,128)} async-done(((f32[4,256,16,256]{3,0,1,2:T(4,128)}), f32[4,256,16,256]{3,0,1,2:T(4,128)}, u32[]{:S(2)}, u32[]{:S(2)}) %all-to-all-start) | async-done | bytes 16777248 | tf_op jit(solution)/shard_map/all_to_all | solution.py:65
  313.8 29.0 %fusion.2 = f32[8,256,4,256]{3,0,2,1:T(8,128)S(1)} fusion(f32[8,256,4,256]{3,2,1,0:T(4,128)} %reshape.591, f32[8,4]{0,1:T(4,128)S(1)} %copy.119, f32[4,256,16,256,1]{3,0,1,2,4:T(4,128)} %bitcast.4, f32[16,4]{0,1:T(4,128)S(1)} %fusion.54, f32[4,16,8]{1,2,0:T(8,128)S(1)} %fusion.43), kind=kOutput, calls=%fused_computation.11 | convolution fusion | flops 1614809088 | bytes 33556864 | tf_op jit(solution)/shard_map/jslc,jxsy->lxcy/dot_general | solution.py:36
  342.8 3.4 copy-done.3
  348.7 4.7 select_select_fusion.3
  353.7 76.1 %all-reduce.12.cloned.1.call-done = f32[256,4,256]{2,1,0:T(4,128)} async-done(((f32[256,4,256]{2,1,0:T(4,128)}), f32[256,4,256]{2,1,0:T(4,128)}) %all-reduce.12.cloned.1.call-update) | async-done | bytes 1048592 | tf_op jit(solution)/shard_map/psum | solution.py:15
  429.8 143.5 %all-reduce.10.cloned.1.call-done = f32[8,256,256]{2,0,1:T(8,128)} async-done(((f32[8,256,256]{2,0,1:T(8,128)}), f32[8,256,256]{2,0,1:T(8,128)}) %all-reduce.10.cloned.1.call-update) | async-done | bytes 2097168 | tf_op jit(solution)/shard_map/psum | solution.py:15
  573.3 11.0 convolution_subtract_fusion.3
  585.1 3.4 copy-done.4
  590.9 3.1 select_select_fusion.2
  594.5 80.2 %all-reduce.16.cloned.1.call-done = f32[256,4,256]{2,1,0:T(4,128)} async-done(((f32[256,4,256]{2,1,0:T(4,128)}), f32[256,4,256]{2,1,0:T(4,128)}) %all-reduce.16.cloned.1.call-update) | async-done | bytes 1048592 | tf_op jit(solution)/shard_map/psum | solution.py:15
  674.7 143.4 %all-reduce.14.cloned.1.call-done = f32[8,256,256]{2,0,1:T(8,128)} async-done(((f32[8,256,256]{2,0,1:T(8,128)}), f32[8,256,256]{2,0,1:T(8,128)}) %all-reduce.14.cloned.1.call-update) | async-done | bytes 2097168 | tf_op jit(solution)/shard_map/psum | solution.py:15
  818.1 11.0 convolution_subtract_fusion.2
  829.9 3.4 copy-done.5
  835.8 3.1 select_select_fusion.1
  839.0 80.6 %all-reduce.20.cloned.1.call-done = f32[256,4,256]{2,1,0:T(4,128)} async-done(((f32[256,4,256]{2,1,0:T(4,128)}), f32[256,4,256]{2,1,0:T(4,128)}) %all-reduce.20.cloned.1.call-update) | async-done | bytes 1048592 | tf_op jit(solution)/shard_map/psum | solution.py:15
  919.6 143.4 %all-reduce.18.cloned.1.call-done = f32[8,256,256]{2,0,1:T(8,128)} async-done(((f32[8,256,256]{2,0,1:T(8,128)}), f32[8,256,256]{2,0,1:T(8,128)}) %all-reduce.18.cloned.1.call-update) | async-done | bytes 2097168 | tf_op jit(solution)/shard_map/psum | solution.py:15
  1063.0 11.0 convolution_subtract_fusion.1
  1074.8 3.4 copy-done.6
  1080.8 3.1 select_select_fusion
  1083.9 80.5 %all-reduce.24.cloned.1.call-done = f32[256,4,256]{2,1,0:T(4,128)} async-done(((f32[256,4,256]{2,1,0:T(4,128)}), f32[256,4,256]{2,1,0:T(4,128)}) %all-reduce.24.cloned.1.call-update) | async-done | bytes 1048592 | tf_op jit(solution)/shard_map/psum | solution.py:15
  1164.5 143.5 %all-reduce.22.cloned.1.call-done = f32[8,256,256]{2,0,1:T(8,128)} async-done(((f32[8,256,256]{2,0,1:T(8,128)}), f32[8,256,256]{2,0,1:T(8,128)}) %all-reduce.22.cloned.1.call-update) | async-done | bytes 2097168 | tf_op jit(solution)/shard_map/psum | solution.py:15
  1308.0 12.1 convolution_subtract_fusion
  1320.1 3.2 fusion.7
  1323.3 9.8 copy.182
  1333.1 8.9 copy.192
  (104 shorter events, 22.8 us)
Async XLA Ops:
  6.5 48.2 %copy-start = (s32[64,64]{1,0:T(8,128)S(1)}, s32[64,64]{1,0:T(8,128)}, u32[]{:S(2)}) copy-start(s32[64,64]{1,0:T(8,128)} %param.17) | copy-start | bytes 49156
  47.4 266.4 %all-to-all-start = ((f32[4,256,16,256]{3,0,1,2:T(4,128)}), f32[4,256,16,256]{3,0,1,2:T(4,128)}, u32[]{:S(2)}, u32[]{:S(2)}) async-start(f32[4,256,16,256]{3,0,1,2:T(4,128)} %copy.115), calls=%async_computation | async-start | bytes 33554432 | tf_op jit(solution)/shard_map/all_to_all | solution.py:65
  54.3 375.4 %all-reduce.12.cloned.1.call-start = ((), (), s32[]{:S(2)}) async-start(), calls=%async_computation.2 | async-start | bytes 2097152 | tf_op jit(solution)/shard_map/psum | solution.py:15
  54.7 0.9 copy-start.2
  342.8 3.4 copy-start.3
  347.1 1.5 copy-start.11
  348.6 224.7 %all-reduce.10.cloned.1.call-start = ((), (), s32[]{:S(2)}) async-start(), calls=%async_computation.1 | async-start | bytes 4194304 | tf_op jit(solution)/shard_map/psum | solution.py:15
  353.4 321.3 %all-reduce.16.cloned.1.call-start = ((), (), s32[]{:S(2)}) async-start(), calls=%async_computation.4 | async-start | bytes 2097152 | tf_op jit(solution)/shard_map/psum | solution.py:15
  573.3 11.0 copy-start.7
  585.1 3.4 copy-start.4
  590.9 227.2 %all-reduce.14.cloned.1.call-start = ((), (), s32[]{:S(2)}) async-start(), calls=%async_computation.3 | async-start | bytes 4194304 | tf_op jit(solution)/shard_map/psum | solution.py:15
  594.1 325.5 %all-reduce.20.cloned.1.call-start = ((), (), s32[]{:S(2)}) async-start(), calls=%async_computation.6 | async-start | bytes 2097152 | tf_op jit(solution)/shard_map/psum | solution.py:15
  818.1 11.0 copy-start.8
  829.9 3.4 copy-start.5
  835.7 227.3 %all-reduce.18.cloned.1.call-start = ((), (), s32[]{:S(2)}) async-start(), calls=%async_computation.5 | async-start | bytes 4194304 | tf_op jit(solution)/shard_map/psum | solution.py:15
  838.9 325.6 %all-reduce.24.cloned.1.call-start = ((), (), s32[]{:S(2)}) async-start(), calls=%async_computation.8 | async-start | bytes 2097152 | tf_op jit(solution)/shard_map/psum | solution.py:15
  1063.0 11.0 copy-start.9
  1074.8 3.4 copy-start.6
  1080.6 227.4 %all-reduce.22.cloned.1.call-start = ((), (), s32[]{:S(2)}) async-start(), calls=%async_computation.7 | async-start | bytes 4194304 | tf_op jit(solution)/shard_map/psum | solution.py:15
  1308.0 12.1 copy-start.10
  1333.1 8.9 copy-start.1
Sparse Core Ops, SparseCore 0:
  348.7 80.9 all-reduce.11
  432.3 140.9 all-reduce.9
  591.0 83.6 all-reduce.15
  677.1 140.9 all-reduce.13
  835.8 83.7 all-reduce.19
  922.0 140.9 all-reduce.17
  1080.7 83.7 all-reduce.23
  1167.0 140.9 all-reduce.21
where the time goes:
time: 1360 us; the launch traced here: 1350 us
  waiting for transfers between devices  1130 us (83%)
  matrix products  87.9 us (6%)
  local copies, waits for them, and re-layouts  84.6 us (6%)
  other arithmetic  22 us (2%)
  between operations  14.1 us (1%)
    psum x8, waiting for transfers between devices, from_root(): return lax.psum(block, axis)  891 us
    all_to_all x1, waiting for transfers between devices, body(): lax.all_to_all(outgoing, 'col', split_axis=2, concat_axis=2, tiled=True)  241 us
    dot_general x4, matrix products, body(): jnp.einsum('lxz,zcy->lxcy', received_lower, upper_part, precision=exact_m...  44.9 us
    dot_general x1, matrix products, deposit(): return jnp.einsum('jslc,jxsy->lxcy', weight, values, precision=exact_mode)  29 us
  transfers between devices with their start and end apart: 9, of which 9 were waited for; matrix products, arithmetic and copies ran while one was open for 2% of the time, Pallas kernels for 0%

commit v1 on v0

v1 whole, which is shorter than its diff:
```python
import functools

import jax
import jax.numpy as jnp
from jax import lax
from jax.experimental import pallas as pl
from jax.experimental.pallas import tpu as pltpu
from jax.sharding import PartitionSpec as P

BS = 256
K = 4
MESH = pl.DeviceIdType.MESH
f32 = jnp.float32
bf16 = jnp.bfloat16


def place(imap, child, g, h, z, core):
    t = imap[child, 8 * g] - 8 * g
    first = (core + t) % 2
    start = (4 * g + (t + first) // 2) % 8
    m = (z + 8 - start) % 4
    half = ((start + m) % 8) // 4
    block = 8 * g + t + first + 2 * m
    return half == h, block // 16


def local_row(imap, child, jj, r):
    t = imap[child, 8 * jj] - 8 * jj
    return jj + (t + (r + 64 - t) % 8) // 8


def exchange_kernel(
    imap, mask, contrib, front,
    R, X, LR, UR, CR,
    cv, SP, M0, M1, M2, M3, S, PC, PR, FC, FR, RBr, RBx, RCr, RCx,
    ld, ldf, cs, cr, zs, zr, xs, xr, own,
    ldb, ldc, lcopy, Ls, Lr, Lxs, Lcs, Lcr, L3s,
    Us, Ur, Ups, ucopy, Cs, Cr, Cps, ccopy, Ccs, Ccr,
):
    M = [M0, M1, M2, M3]
    r = lax.axis_index("row")
    c = lax.axis_index("col")
    y, e = r // 2, r % 2
    h, z, core = c // 8, (c // 2) % 4, c % 2

    def dev(y_, e_, h_, z_, core_):
        return (2 * y_ + e_, 8 * h_ + 2 * z_ + core_)

    core_peer = dev(y, e, h, z, 1 - core)
    x_peer = dev(y, e, 1 - h, z, core)
    e_peer = dev(y, 1 - e, h, z, core)

    def z_peer(z_):
        return dev(y, e, h, z_, core)

    def y_peer(y_):
        return dev(y_, e, h, z, core)

    def remote(src, dst, ss, rs, to):
        return pltpu.make_async_remote_copy(
            src_ref=src, dst_ref=dst, send_sem=ss, recv_sem=rs, device_id=to, device_id_type=MESH
        )

    def load_c(jj):
        return pltpu.make_async_copy(contrib.at[pl.ds(jj * BS, BS)], cv.at[jj], ld.at[jj])

    for jj in range(4):
        load_c(jj).start()
    is_col_source = (h == 0) & (z < 2)
    is_row_source = r < 4
    load_fc = pltpu.make_async_copy(front.at[:, pl.ds(0, BS)], FC, ldf.at[0])
    load_fr = pltpu.make_async_copy(front.at[pl.ds(0, BS)], FR, ldf.at[1])

    @pl.when(is_col_source)
    def _():
        load_fc.start()

    @pl.when(is_row_source)
    def _():
        load_fr.start()

    barrier = pltpu.get_barrier_semaphore()
    peers = [core_peer, x_peer, e_peer]
    peers += [z_peer((z + d) % 4) for d in (1, 2, 3)]
    peers += [y_peer((y + d) % 4) for d in (1, 3)]
    for p in peers:
        pl.semaphore_signal(barrier, inc=1, device_id=p, device_id_type=MESH)
    pl.semaphore_wait(barrier, len(peers))

    t_own = imap[h, 8 * z] - 8 * z
    odd_mine = (core + t_own) % 2
    start_own = (4 * z + (t_own + odd_mine) // 2) % 8

    def core_copy(jj):
        return remote(SP.at[jj], M[jj].at[pl.ds(2 * core, 2)], cs.at[jj], cr.at[jj], core_peer)

    for jj in range(4):
        load_c(jj).wait()
        for i in range(2):
            even = cv[jj, :, 2 * i * BS:(2 * i + 1) * BS]
            odd = cv[jj, :, (2 * i + 1) * BS:(2 * i + 2) * BS]
            SP[jj, i] = jnp.where(odd_mine == 1, even, odd)
            M[jj][2 * core + i] = jnp.where(odd_mine == 1, odd, even)
        core_copy(jj).start()

    def z_copy(jj, d):
        to = (z + d) % 4
        return remote(S.at[jj, to], R.at[z, jj], zs.at[jj, d], zr.at[jj, z], z_peer(to))

    def z_wait(jj, g):
        remote(S.at[jj, 0], R.at[g, jj], zs.at[jj, 0], zr.at[jj, g], z_peer(g)).wait_recv()

    def own_copy(jj):
        return pltpu.make_async_copy(S.at[jj, z], R.at[z, jj], own.at[jj])

    def x_own(jj):
        return remote(S.at[jj, z], X.at[z, jj], xs.at[jj, z], xr.at[jj, z], x_peer)

    def x_copy(jj, g):
        return remote(R.at[g, jj], X.at[g, jj], xs.at[jj, g], xr.at[jj, g], x_peer)

    def forward_x(jj, d):
        g = (z + d) % 4
        z_wait(jj, g)
        x_copy(jj, g).start()

    for jj in range(4):
        core_copy(jj).wait_recv()
        for to in range(4):
            S[jj, to] = M[jj][(to + 8 - start_own) % 4]
        own_copy(jj).start()
        for d in (1, 3, 2):
            z_copy(jj, d).start()
        if jj == 0:
            x_own(jj).start()

    for d in (1, 3, 2):
        forward_x(0, d)
    for jj in range(1, 4):
        x_own(jj).start()
    for jj in range(4):
        own_copy(jj).wait()

    def u_next(k, half):
        s = k // 2
        d = 1 if half == 0 else -1
        return y_peer((y + 4 + d) % 4)

    def u_copy(k, half, src):
        return remote(
            src, UR.at[k, pl.ds(half * 128, 128)], Us.at[k, half], Ur.at[k, half], u_next(k, half)
        )

    def u_partner(half):
        return remote(
            PR.at[pl.ds(half * 128, 128)], UR.at[r, pl.ds(half * 128, 128)],
            Ups.at[half], Ur.at[r, half], e_peer,
        )

    own_u = pltpu.make_async_copy(PR, UR.at[jnp.minimum(r, 3)], ucopy.at[0])

    @pl.when(is_row_source)
    def _():
        for g in range(4):
            x_copy(0, g).wait_recv()
        for g in range(4):
            pltpu.make_async_copy(R.at[g, 0], RBr.at[g], ldb.at[0, g]).start()
            pltpu.make_async_copy(X.at[g, 0], RBx.at[g], ldb.at[1, g]).start()
        load_fr.wait()
        for g in range(4):
            pltpu.make_async_copy(R.at[g, 0], RBr.at[g], ldb.at[0, g]).wait()
            pltpu.make_async_copy(X.at[g, 0], RBx.at[g], ldb.at[1, g]).wait()
        row_in = [(local_row(imap, child, 0, r) == 0) for child in (h, 1 - h)]
        hit = []
        for g in range(4):
            for w, child in enumerate((h, 1 - h)):
                lands, lc = place(imap, child, g, h, z, core)
                hit.append((w, g, lands & row_in[w], lc))
        for lc in range(4):
            weights = [(w, g, jnp.where(ok & (at == lc), 1.0, 0.0).astype(f32)) for w, g, ok, at in hit]
            present = mask[r, c + 16 * lc].astype(f32)

            @pl.loop(0, 8)
            def _(q):
                rows = pl.ds(pl.multiple_of(q * 32, 32), 32)
                total = FR[rows, lc * BS:(lc + 1) * BS]
                for w, g, weight in weights:
                    total = total + weight * (RBr if w == 0 else RBx)[g, rows, :]
                PR[rows, lc * BS:(lc + 1) * BS] = total * present
        own_u.start()
        for half in range(2):
            u_partner(half).start()
            u_copy(r, half, PR.at[pl.ds(half * 128, 128)]).start()

    @pl.when(z != 0)
    def _():
        for jj in range(1, 4):
            z_wait(jj, 0)
            x_copy(jj, 0).start()

    panel = 2 * z + core

    def l_next(l):
        return z_peer((z + (1 if l % 2 == 0 else 3)) % 4)

    def l_copy(s, l, src):
        return remote(src, LR.at[2 * s + core, l], Ls.at[s, l], Lr.at[s, l], l_next(l))

    def l_wait(s, l):
        l_copy(s, l, LR.at[2 * s + core, l]).wait_recv()

    def l_x(s, l):
        return remote(
            LR.at[2 * s + core, l], LR.at[2 * s + core, l], Lxs.at[s, l], Lr.at[s, l], x_peer
        )

    def l_x_source(l):
        return remote(PC.at[l], LR.at[panel, l], Lxs.at[z, l], Lr.at[z, l], x_peer)

    def l_core(s, l):
        return remote(
            LR.at[2 * s + core, l], LR.at[2 * s + core, l], Lcs.at[s, l], Lcr.at[s, l], core_peer
        )

    def l_three(s, l, d):
        return remote(
            LR.at[2 * s + core, l], LR.at[2 * s + core, l],
            L3s.at[s, l, d], Lr.at[s, l], z_peer((z + d) % 4),
        )

    shift = [0, 0, 1, 3, 1, 3, 2, 2]
    own_l = pltpu.make_async_copy(PC, LR.at[jnp.minimum(panel, 3)], lcopy.at[0])

    @pl.when(is_col_source)
    def _():
        @pl.when(z == 0)
        def _():
            for jj in range(4):
                if jj > 0:
                    x_copy(jj, 0).wait_recv()

        @pl.when(z != 0)
        def _():
            for jj in range(1, 4):
                x_copy(jj, 0).wait_recv()

        @pl.when(r >= 4)
        def _():
            x_copy(0, 0).wait_recv()

        from_r = pltpu.make_async_copy(R.at[0], RCr, ldc.at[0])
        from_x = pltpu.make_async_copy(X.at[0], RCx, ldc.at[1])
        from_r.start()
        from_x.start()
        load_fc.wait()
        from_r.wait()
        from_x.wait()
        hits = [place(imap, child, 0, h, z, core) for child in (h, 1 - h)]
        rows_at = [[local_row(imap, child, jj, r) for jj in range(4)] for child in (h, 1 - h)]
        for l in range(8):
            present = mask[r + 8 * l, c].astype(f32)
            total = FC[l * BS:(l + 1) * BS, :]
            for w, source in enumerate((RCr, RCx)):
                lands, lc = hits[w]
                index = jnp.int32(0)
                found = jnp.int32(0)
                for jj in range(4):
                    here = (rows_at[w][jj] == l).astype(jnp.int32)
                    index = jnp.where(here > 0, jj, index)
                    found = found + here
                weight = jnp.where(lands & (lc == 0) & (found > 0), 1.0, 0.0).astype(f32)
                total = total + weight * source[index]
            PC[l] = total * present
            l_copy(z, l, PC.at[l]).start()
            if shift[l] == 0:
                l_x_source(l).start()
        own_l.start()

    for jj in range(1, 4):
        for d in (1, 3, 2):
            g = (z + d) % 4

            @pl.when(g != 0)
            def _():
                z_wait(jj, g)
                x_copy(jj, g).start()

    @pl.when(is_col_source)
    def _():
        own_l.wait()

    def at_source(s):
        return (h == 0) & (z == s)

    def column_step(s, l):
        dist = (z + 4 - s) % 4 if l % 2 == 0 else (s + 4 - z) % 4
        cross_z = (s + shift[l]) % 4

        @pl.when(jnp.logical_not(at_source(s)))
        def _():
            l_wait(s, l)

        @pl.when(h == 0)
        def _():
            @pl.when((dist > 0) & (dist < 3))
            def _():
                l_copy(s, l, LR.at[2 * s + core, l]).start()

            if shift[l] != 0:
                @pl.when(z == cross_z)
                def _():
                    l_x(s, l).start()

        @pl.when((h == 1) & (z == cross_z))
        def _():
            for d in (1, 3, 2):
                l_three(s, l, d).start()

        l_core(s, l).start()

    def c_next(s):
        return y_peer((y + (1 if s == 0 else 3)) % 4)

    def c_copy(k, s, src):
        return remote(src, CR.at[k, core, s], Cs.at[k, s], Cr.at[k, s], c_next(s))

    def c_partner(s):
        return remote(LR.at[2 * s + core, 0], CR.at[r, core, s], Cps.at[s], Cr.at[r, s], e_peer)

    def c_own(s):
        return pltpu.make_async_copy(
            LR.at[2 * s + core, 0], CR.at[jnp.minimum(r, 3), core, s], ccopy.at[s]
        )

    def c_core(k):
        return remote(CR.at[k, core], CR.at[k, core], Ccs.at[k], Ccr.at[k], core_peer)

    def ring_dist(k, way):
        s = k // 2
        return (y + 4 - s) % 4 if way == 0 else (s + 4 - y) % 4

    def row_step(k, half):
        dist = ring_dist(k, half)

        @pl.when(r != k)
        def _():
            u_copy(k, half, UR.at[k, pl.ds(half * 128, 128)]).wait_recv()

            @pl.when(dist < 3)
            def _():
                u_copy(k, half, UR.at[k, pl.ds(half * 128, 128)]).start()

    def corner_step(k, s):
        dist = ring_dist(k, s)

        @pl.when(r != k)
        def _():
            c_copy(k, s, CR.at[k, core, s]).wait_recv()

            @pl.when(dist < 3)
            def _():
                c_copy(k, s, CR.at[k, core, s]).start()

    for s in range(2):
        column_step(s, 0)

    @pl.when(is_row_source)
    def _():
        for s in range(2):
            c_own(s).start()
            c_partner(s).start()
            c_copy(r, s, LR.at[2 * s + core, 0]).start()

    for s in range(2):
        column_step(s, 1)
    for k in range(4):
        for half in range(2):
            row_step(k, half)
    for l in (2, 3):
        for s in range(2):
            column_step(s, l)
    for k in range(4):
        for s in range(2):
            corner_step(k, s)

        @pl.when(r == k)
        def _():
            for s in range(2):
                c_own(s).wait()

        c_core(k).start()
    for l in (4, 5, 6, 7):
        for s in range(2):
            column_step(s, l)

    for jj in range(4):
        core_copy(jj).wait_send()
        for d in (1, 2, 3):
            z_copy(jj, d).wait_send()
        for g in range(4):
            x_copy(jj, g).wait_send()

    for g in range(4):
        for jj in range(4):
            done = jnp.bool_(False)
            if jj == 0:
                done = is_row_source | ((g == 0) & is_col_source)
            elif g == 0:
                done = is_col_source

            @pl.when(jnp.logical_not(done))
            def _():
                x_copy(jj, g).wait_recv()

    @pl.when(is_row_source)
    def _():
        own_u.wait()
        for half in range(2):
            u_partner(half).wait_send()
            u_copy(r, half, PR.at[pl.ds(half * 128, 128)]).wait_send()
        for s in range(2):
            c_partner(s).wait_send()
            c_copy(r, s, LR.at[2 * s + core, 0]).wait_send()
    for k in range(4):
        for way in range(2):
            dist = ring_dist(k, way)

            @pl.when((r != k) & (dist < 3))
            def _():
                u_copy(k, way, UR.at[k, pl.ds(way * 128, 128)]).wait_send()
                c_copy(k, way, CR.at[k, core, way]).wait_send()

        c_core(k).wait()
    for s in range(2):
        for l in range(8):
            dist = (z + 4 - s) % 4 if l % 2 == 0 else (s + 4 - z) % 4
            cross_z = (s + shift[l]) % 4

            @pl.when(h == 0)
            def _():
                @pl.when(dist < 3)
                def _():
                    l_copy(s, l, LR.at[2 * s + core, l]).wait_send()

                @pl.when(z == cross_z)
                def _():
                    l_x(s, l).wait_send()

            @pl.when((h == 1) & (z == cross_z))
            def _():
                for d in (1, 3, 2):
                    l_three(s, l, d).wait_send()

            l_core(s, l).wait()


def split(a):
    hi = a.astype(bf16)
    return hi, (a - hi.astype(f32)).astype(bf16)


def dot3(a, b):
    ah, al = a
    bh, bl = b
    d = functools.partial(jnp.dot, preferred_element_type=f32)
    return d(ah, bh) + (d(ah, bl) + d(al, bh))


def panel_kernel(pos, CR, UR, pinv, Vh, Vl, frow, PB, U):
    r, c = pos[0], pos[1]
    for k in range(4):
        for j in range(4):
            PB[k * BS:(k + 1) * BS, j * BS:(j + 1) * BS] = CR[k, j % 2, j // 2]
        U[k * BS:(k + 1) * BS, :] = UR[k]
    for k in range(3):
        at, rest = k * BS, (k + 1) * BS
        lower = dot3(split(PB[rest:, at:rest]), split(pinv[k]))
        PB[rest:, at:rest] = lower
        low = split(lower)
        PB[rest:, rest:] = PB[rest:, rest:] - dot3(low, split(PB[at:rest, rest:]))
        U[rest:, :] = U[rest:, :] - dot3(low, split(U[at:rest, :]))

    @pl.when(r < 4)
    def _():
        rows = pl.ds(pl.multiple_of(r * BS, BS), BS)
        frow[...] = U[rows, :]

        @pl.when(c < 4)
        def _():
            frow[:, 0:BS] = PB[rows, pl.ds(pl.multiple_of(c * BS, BS), BS)]

    @pl.when(r >= 4)
    def _():
        frow[...] = jnp.zeros_like(frow)

    @pl.when(c < 4)
    def _():
        on = lax.broadcasted_iota(jnp.int32, (K * BS, BS), 0)
        across = lax.broadcasted_iota(jnp.int32, (K * BS, BS), 1)
        U[:, 0:BS] = jnp.where(on == across + c * BS, -1.0, 0.0).astype(f32)

    for m in range(3, -1, -1):
        at, rest = m * BS, (m + 1) * BS
        total = U[at:rest, :]
        if m < 3:
            total = total - dot3(split(PB[at:rest, rest:]), (Vh[rest:, :], Vl[rest:, :]))
        vh, vl = split(dot3(split(pinv[m]), split(total)))
        Vh[at:rest, :] = vh
        Vl[at:rest, :] = vl


def child_row(imap, pos, child, l):
    index = jnp.int32(0)
    found = jnp.int32(0)
    for jj in range(4):
        here = (local_row(imap, child, jj, pos[0]) == l).astype(jnp.int32)
        index = jnp.where(here > 0, jj, index)
        found = found + here
    return index, found


def update_kernel(imap, mask, pos, F, LRl, R, X, Vh, Vl, frow, out, acc, ah, al):
    l = pl.program_id(0)
    r, c = pos[0], pos[1]
    h, z, core = c // 8, (c // 2) % 4, c % 2
    for lc in range(4):
        acc[lc] = F[:, lc * BS:(lc + 1) * BS]
    for child, source in ((h, R), (1 - h, X)):
        _, found = child_row(imap, pos, child, l)
        for g in range(4):
            lands, lc = place(imap, child, g, h, z, core)

            @pl.when(lands & (found > 0))
            def _():
                acc[lc] = acc[lc] + source[g, 0]
    for p in range(4):
        hi, lo = split(LRl[p, 0])
        ah[:, p * BS:(p + 1) * BS] = hi
        al[:, p * BS:(p + 1) * BS] = lo
    for lc in range(4):
        present = mask[r + 8 * l, c + 16 * lc].astype(f32)
        if lc == 0:
            present = present * (c >= 4).astype(f32)
        cols = slice(lc * BS, (lc + 1) * BS)
        product = dot3((ah[...], al[...]), (Vh[:, cols], Vl[:, cols]))
        out[:, cols] = acc[lc] * present - product

    @pl.when((l == 0) & (r < 4))
    def _():
        out[...] = frow[...]


def body(front, contrib, pivot_inverse, index_map, fill_mask):
    r = lax.axis_index("row")
    c = lax.axis_index("col")
    pos = jnp.stack([r, c]).astype(jnp.int32)
    any_ = pl.BlockSpec(memory_space=pl.ANY)
    smem = pl.BlockSpec(memory_space=pltpu.SMEM)
    vmem = pl.BlockSpec(memory_space=pltpu.VMEM)
    V = pltpu.VMEM
    dma = pltpu.SemaphoreType.DMA
    blk = (BS, BS)
    R, X, LR, UR, CR = pl.pallas_call(
        exchange_kernel,
        out_shape=[
            jax.ShapeDtypeStruct((4, 4) + blk, f32),
            jax.ShapeDtypeStruct((4, 4) + blk, f32),
            jax.ShapeDtypeStruct((4, 8) + blk, f32),
            jax.ShapeDtypeStruct((4, BS, 4 * BS), f32),
            jax.ShapeDtypeStruct((4, 2, 2) + blk, f32),
        ],
        in_specs=[smem, smem, any_, any_],
        out_specs=[any_] * 5,
        scratch_shapes=[
            V((4, BS, 4 * BS), f32), V((4, 2) + blk, f32),
            V((4,) + blk, f32), V((4,) + blk, f32), V((4,) + blk, f32), V((4,) + blk, f32),
            V((4, 4) + blk, f32), V((8,) + blk, f32), V((BS, 4 * BS), f32),
            V((8 * BS, BS), f32), V((BS, 4 * BS), f32),
            V((4,) + blk, f32), V((4,) + blk, f32), V((4,) + blk, f32), V((4,) + blk, f32),
            dma((4,)), dma((2,)), dma((4,)), dma((4,)), dma((4, 4)), dma((4, 4)), dma((4, 4)),
            dma((4, 4)), dma((4,)),
            dma((2, 4)), dma((2,)), dma((1,)), dma((2, 8)), dma((2, 8)), dma((2, 8)), dma((2, 8)),
            dma((2, 8)), dma((2, 8, 4)),
            dma((4, 2)), dma((4, 2)), dma((2,)), dma((1,)), dma((4, 2)), dma((4, 2)), dma((2,)),
            dma((2,)), dma((4,)), dma((4,)),
        ],
        compiler_params=pltpu.CompilerParams(
            collective_id=0, has_side_effects=True, vmem_limit_bytes=48 * 2**20
        ),
        name="exchange",
    )(index_map, fill_mask, contrib, front)

    Vh, Vl, frow = pl.pallas_call(
        panel_kernel,
        out_shape=[
            jax.ShapeDtypeStruct((4 * BS, 4 * BS), bf16),
            jax.ShapeDtypeStruct((4 * BS, 4 * BS), bf16),
            jax.ShapeDtypeStruct((BS, 4 * BS), f32),
        ],
        in_specs=[smem, vmem, vmem, vmem],
        out_specs=[vmem] * 3,
        scratch_shapes=[V((4 * BS, 4 * BS), f32), V((4 * BS, 4 * BS), f32)],
        compiler_params=pltpu.CompilerParams(vmem_limit_bytes=56 * 2**20),
        name="panel",
    )(pos, CR, UR, pivot_inverse)

    def child_spec(own):
        def index(l, imap, mask, pos):
            child = pos[1] // 8
            if not own:
                child = 1 - child
            return 0, child_row(imap, pos, child, l)[0], 0, 0

        return pl.BlockSpec((4, 1) + blk, index)

    return pl.pallas_call(
        update_kernel,
        out_shape=jax.ShapeDtypeStruct(front.shape, f32),
        grid_spec=pltpu.PrefetchScalarGridSpec(
            num_scalar_prefetch=3,
            grid=(8,),
            in_specs=[
                pl.BlockSpec((BS, 4 * BS), lambda l, *_: (l, 0)),
                pl.BlockSpec((4, 1) + blk, lambda l, *_: (0, l, 0, 0)),
                child_spec(True),
                child_spec(False),
                pl.BlockSpec((4 * BS, 4 * BS), lambda l, *_: (0, 0)),
                pl.BlockSpec((4 * BS, 4 * BS), lambda l, *_: (0, 0)),
                pl.BlockSpec((BS, 4 * BS), lambda l, *_: (0, 0)),
            ],
            out_specs=pl.BlockSpec((BS, 4 * BS), lambda l, *_: (l, 0)),
            scratch_shapes=[V((4,) + blk, f32), V((BS, 4 * BS), bf16), V((BS, 4 * BS), bf16)],
        ),
        compiler_params=pltpu.CompilerParams(vmem_limit_bytes=48 * 2**20),
        name="update",
    )(index_map, fill_mask, pos, front, LR, R, X, Vh, Vl, frow)


def solution(mesh):
    in_specs = (P("row", "col"), P("row", "col"), P(), P(), P())
    out_specs = P("row", "col")
    return jax.shard_map(body, mesh=mesh, in_specs=in_specs, out_specs=out_specs, check_vma=False)
```

time: 1360 us -> 554 us (0.41)
  waiting for transfers between devices: 1130 us -> 0 us
  Pallas kernels: 0 us -> 539 us
  matrix products: 87.9 us -> 0 us
  local copies, waits for them, and re-layouts: 84.6 us -> 7.77 us
  other arithmetic: 22 us -> 0.58 us
  between operations: 14.1 us -> 0.04 us
    psum x8 -> x0, waiting for transfers between devices: 891 us -> none  [from_root(): return lax.psum(block, axis)]
    pallas_call x0 -> x3, Pallas kernels: none -> 539 us  [the longest x1 498 us: body(): pl.pallas_call(exchange_kernel, out_shape=[jax.ShapeDtypeStruct((4, 4) +...]
    all_to_all x1 -> x0, waiting for transfers between devices: 241 us -> none  [body(): lax.all_to_all(outgoing, 'col', split_axis=2, concat_axis=2, tiled=True)]
    dot_general x9 -> x0, matrix products: 87.9 us -> none  [the longest x4 44.9 us: body(): jnp.einsum('lxz,zcy->lxcy', received_lower, upper_part, precision=exact_m...]
    reshape x4 -> x0, local copies, waits for them, and re-layouts: 30.8 us -> none  [the longest x1 10.5 us: body(): front.reshape(row_blocks, BS, col_blocks, BS) + assembled]
    gather x8 -> x0, local copies, waits for them, and re-layouts: 14.8 us -> none  [the longest x1 9.9 us: body(): outgoing = jnp.take(stripes, chosen, axis=2, mode='fill', fill_value=0.0)]
    select_n x14 -> x0, other arithmetic: 14.7 us -> none  [the longest x2 7.22 us: body(): outgoing = jnp.take(stripes, chosen, axis=2, mode='fill', fill_value=0.0)]
    unnamed x25 -> x18, local copies, waits for them, and re-layouts: 22.5 us -> 7.77 us
  transfers between devices with their start and end apart: 9 -> 0, of which waited for: 9 -> 0; matrix products, arithmetic and copies ran while one was open for 2% -> 0% of each run, Pallas kernels for 0% -> 0%
where the time goes in v1:
time: 554 us; the launch traced here: 547 us
  Pallas kernels  539 us (97%)
  local copies, waits for them, and re-layouts  7.77 us (1%)
    pallas_call x1, Pallas kernels, body(): pl.pallas_call(exchange_kernel, out_shape=[jax.ShapeDtypeStruct((4, 4) +...  498 us
    pallas_call x1, Pallas kernels, body(): pl.pallas_call(update_kernel, out_shape=jax.ShapeDtypeStruct(front.shape,...  24.5 us
    pallas_call x1, Pallas kernels, body(): pl.pallas_call(panel_kernel, out_shape=[jax.ShapeDtypeStruct((4 * BS, 4 *...  16.8 us

profile of v1, /device:TPU:118, one launch (start us, length us, event | category | flops | bytes accessed | tf_op | source)
XLA Modules:
  0.0 547.4 jit_solution(18303053921856406821)
XLA Ops:
  0.0 0.6 pad_add_fusion.pos
  0.6 0.0 copy-start.4
  0.6 0.8 copy-done.4
  1.3 0.0 copy-start.6
  1.3 0.7 copy-done.6
  2.0 497.8 %exchange.1 = (f32[4,4,256,256]{3,2,1,0:T(8,128)S(1)}, f32[4,4,256,256]{3,2,1,0:T(8,128)}, f32[4,8,256,256]{3,2,1,0:T(8,128)}, f32[4,256,1024]{2,1,0:T(8,128)}, f32[4,2,2,256,256]{4,3,2,1,0:T(8,128)}) custom-call(s32[2,32]{1,0:T(2,128)S(1)} %copy-done.6, s32[64,64]{1,0:T(8,128)S(1)} %copy-done.4, f32[1024,1024]{1,0:T(8,128)} %contrib.1, f32[2048,1024]{1,0:T(8,128)} %F.1), custom_call_target="tpu_custom_call" | custom-call | tf_op jit(solution)/shard_map/exchange/pallas_call | solution.py:563
  499.8 0.0 copy-start
  499.8 1.9 copy-done
  501.7 0.0 copy-start.5
  501.7 0.0 copy-start.7
  501.8 0.0 copy-start.8
  501.8 16.8 %panel.1 = (bf16[1024,1024]{1,0:T(8,128)(2,1)}, bf16[1024,1024]{1,0:T(8,128)(2,1)}, f32[256,1024]{1,0:T(8,128)}) custom-call(s32[2]{0:T(128)} %pad_add_fusion.pos, f32[4,2,2,256,256]{4,3,2,1,0:T(8,128)} %get-tuple-element.16.CR, f32[4,256,1024]{2,1,0:T(8,128)} %get-tuple-element.17.UR, f32[4,256,256]{2,1,0:T(8,128)} %pinv.1), custom_call_target="tpu_custom_call" | custom-call | tf_op jit(solution)/shard_map/panel/pallas_call | solution.py:593
  518.5 0.0 copy-done.5
  518.5 0.0 copy-done.7
  518.5 0.0 copy-done.8
  518.5 0.0 copy-start.1
  518.5 1.6 copy-done.1
  520.1 0.0 copy-start.2
  520.1 1.6 copy-done.2
  521.7 0.0 copy-start.3
  521.7 1.2 copy-done.3
  522.9 24.5 %update.1 = f32[2048,1024]{1,0:T(8,128)} custom-call(s32[2,32]{1,0:T(2,128)S(1)} %copy-done.7, s32[64,64]{1,0:T(8,128)S(1)} %copy-done.5, s32[2]{0:T(128)S(1)} %copy-done.8, f32[2048,1024]{1,0:T(8,128)} %F.1, f32[4,8,256,256]{3,2,1,0:T(8,128)} %get-tuple-element.13.LRl, f32[4,4,256,256]{3,2,1,0:T(8,128)} %copy-done, f32[4,4,256,256]{3,2,1,0:T(8,128)} %get-tuple-element.15.X, ...), custom_call_target="tpu_custom_call" | custom-call | tf_op jit(solution)/shard_map/update/pallas_call | solution.py:616
Async XLA Ops:
  0.6 0.8 copy-start.4
  1.3 0.7 copy-start.6
  499.8 1.9 copy-start
  501.7 16.8 %copy-start.5 = (s32[64,64]{1,0:T(8,128)S(1)}, s32[64,64]{1,0:T(8,128)}, u32[]{:S(2)}) copy-start(s32[64,64]{1,0:T(8,128)} %mask.3) | copy-start | bytes 49156
  501.7 16.8 %copy-start.7 = (s32[2,32]{1,0:T(2,128)S(1)}, s32[2,32]{1,0:T(2,128)}, u32[]{:S(2)}) copy-start(s32[2,32]{1,0:T(2,128)} %imap.3) | copy-start | bytes 772
  501.8 16.8 %copy-start.8 = (s32[2]{0:T(128)S(1)}, s32[2]{0:T(128)}, u32[]{:S(2)}) copy-start(s32[2]{0:T(128)} %pad_add_fusion.pos) | copy-start | bytes 28
  518.5 1.6 copy-start.1
  520.1 1.6 copy-start.2
  521.7 1.2 copy-start.3

commit v2 on v1

--- a/solution.py
+++ b/solution.py
@@ -9,6 +9,8 @@
 
 BS = 256
 K = 4
+FREE = False
+PARTS = "XULC"
 MESH = pl.DeviceIdType.MESH
 f32 = jnp.float32
 bf16 = jnp.bfloat16
@@ -30,7 +32,7 @@
 
 
 def exchange_kernel(
-    imap, mask, contrib, front,
+    free, parts, imap, mask, contrib, front,
     R, X, LR, UR, CR,
     cv, SP, M0, M1, M2, M3, S, PC, PR, FC, FR, RBr, RBx, RCr, RCx,
     ld, ldf, cs, cr, zs, zr, xs, xr, own,
@@ -64,10 +66,12 @@
     def load_c(jj):
         return pltpu.make_async_copy(contrib.at[pl.ds(jj * BS, BS)], cv.at[jj], ld.at[jj])
 
-    for jj in range(4):
+    for jj in range(4) if "X" in parts else ():
         load_c(jj).start()
-    is_col_source = (h == 0) & (z < 2)
-    is_row_source = r < 4
+    has = {name: name in parts for name in "XULC"}
+    never = jnp.bool_(False)
+    is_col_source = (h == 0) & (z < 2) if has["L"] else never
+    is_row_source = r < 4 if has["U"] else never
     load_fc = pltpu.make_async_copy(front.at[:, pl.ds(0, BS)], FC, ldf.at[0])
     load_fr = pltpu.make_async_copy(front.at[pl.ds(0, BS)], FR, ldf.at[1])
 
@@ -94,15 +98,6 @@
     def core_copy(jj):
         return remote(SP.at[jj], M[jj].at[pl.ds(2 * core, 2)], cs.at[jj], cr.at[jj], core_peer)
 
-    for jj in range(4):
-        load_c(jj).wait()
-        for i in range(2):
-            even = cv[jj, :, 2 * i * BS:(2 * i + 1) * BS]
-            odd = cv[jj, :, (2 * i + 1) * BS:(2 * i + 2) * BS]
-            SP[jj, i] = jnp.where(odd_mine == 1, even, odd)
-            M[jj][2 * core + i] = jnp.where(odd_mine == 1, odd, even)
-        core_copy(jj).start()
-
     def z_copy(jj, d):
         to = (z + d) % 4
         return remote(S.at[jj, to], R.at[z, jj], zs.at[jj, d], zr.at[jj, z], z_peer(to))
@@ -124,79 +119,97 @@
         z_wait(jj, g)
         x_copy(jj, g).start()
 
-    for jj in range(4):
+    def swap_cores():
+        for jj in range(4):
+            load_c(jj).wait()
+            for i in range(2):
+                even = cv[jj, :, 2 * i * BS:(2 * i + 1) * BS]
+                odd = cv[jj, :, (2 * i + 1) * BS:(2 * i + 2) * BS]
+                SP[jj, i] = jnp.where(odd_mine == 1, even, odd)
+                M[jj][2 * core + i] = jnp.where(odd_mine == 1, odd, even)
+            core_copy(jj).start()
+
+    def arrange(jj):
         core_copy(jj).wait_recv()
         for to in range(4):
             S[jj, to] = M[jj][(to + 8 - start_own) % 4]
         own_copy(jj).start()
         for d in (1, 3, 2):
             z_copy(jj, d).start()
-        if jj == 0:
-            x_own(jj).start()
-
-    for d in (1, 3, 2):
-        forward_x(0, d)
-    for jj in range(1, 4):
-        x_own(jj).start()
-    for jj in range(4):
-        own_copy(jj).wait()
-
-    def u_next(k, half):
-        s = k // 2
-        d = 1 if half == 0 else -1
-        return y_peer((y + 4 + d) % 4)
-
-    def u_copy(k, half, src):
+
+    def own_waits():
+        for jj in range(4):
+            own_copy(jj).wait()
+
+    def y_next(way):
+        return y_peer((y + (1 if way == 0 else 3)) % 4)
+
+    def u_rows(way, q):
+        return pl.ds(way * 128 + q * 64, 64)
+
+    def u_copy(k, way, q, src):
         return remote(
-            src, UR.at[k, pl.ds(half * 128, 128)], Us.at[k, half], Ur.at[k, half], u_next(k, half)
+            src, UR.at[k, u_rows(way, q)], Us.at[k, way, q], Ur.at[k, way, q], y_next(way)
         )
 
-    def u_partner(half):
+    def u_held(k, way, q):
+        return UR.at[k, u_rows(way, q)]
+
+    def u_partner(way, q):
         return remote(
-            PR.at[pl.ds(half * 128, 128)], UR.at[r, pl.ds(half * 128, 128)],
-            Ups.at[half], Ur.at[r, half], e_peer,
+            PR.at[u_rows(way, q)], UR.at[r, u_rows(way, q)],
+            Ups.at[way, q], Ur.at[r, way, q], e_peer,
         )
 
     own_u = pltpu.make_async_copy(PR, UR.at[jnp.minimum(r, 3)], ucopy.at[0])
 
-    @pl.when(is_row_source)
-    def _():
-        for g in range(4):
-            x_copy(0, g).wait_recv()
-        for g in range(4):
-            pltpu.make_async_copy(R.at[g, 0], RBr.at[g], ldb.at[0, g]).start()
-            pltpu.make_async_copy(X.at[g, 0], RBx.at[g], ldb.at[1, g]).start()
-        load_fr.wait()
-        for g in range(4):
-            pltpu.make_async_copy(R.at[g, 0], RBr.at[g], ldb.at[0, g]).wait()
-            pltpu.make_async_copy(X.at[g, 0], RBx.at[g], ldb.at[1, g]).wait()
-        row_in = [(local_row(imap, child, 0, r) == 0) for child in (h, 1 - h)]
-        hit = []
-        for g in range(4):
-            for w, child in enumerate((h, 1 - h)):
-                lands, lc = place(imap, child, g, h, z, core)
-                hit.append((w, g, lands & row_in[w], lc))
-        for lc in range(4):
-            weights = [(w, g, jnp.where(ok & (at == lc), 1.0, 0.0).astype(f32)) for w, g, ok, at in hit]
-            present = mask[r, c + 16 * lc].astype(f32)
-
-            @pl.loop(0, 8)
-            def _(q):
-                rows = pl.ds(pl.multiple_of(q * 32, 32), 32)
-                total = FR[rows, lc * BS:(lc + 1) * BS]
-                for w, g, weight in weights:
-                    total = total + weight * (RBr if w == 0 else RBx)[g, rows, :]
-                PR[rows, lc * BS:(lc + 1) * BS] = total * present
+    def send_row_panel():
         own_u.start()
-        for half in range(2):
-            u_partner(half).start()
-            u_copy(r, half, PR.at[pl.ds(half * 128, 128)]).start()
-
-    @pl.when(z != 0)
-    def _():
-        for jj in range(1, 4):
-            z_wait(jj, 0)
-            x_copy(jj, 0).start()
+        for q in range(2):
+            for way in range(2):
+                u_partner(way, q).start()
+                u_copy(r, way, q, PR.at[u_rows(way, q)]).start()
+
+    def make_row_panel():
+        @pl.when(is_row_source)
+        def _():
+            for g in range(4):
+                x_copy(0, g).wait_recv()
+            for g in range(4):
+                pltpu.make_async_copy(R.at[g, 0], RBr.at[g], ldb.at[0, g]).start()
+                pltpu.make_async_copy(X.at[g, 0], RBx.at[g], ldb.at[1, g]).start()
+            load_fr.wait()
+            for g in range(4):
+                pltpu.make_async_copy(R.at[g, 0], RBr.at[g], ldb.at[0, g]).wait()
+                pltpu.make_async_copy(X.at[g, 0], RBx.at[g], ldb.at[1, g]).wait()
+            row_in = [(local_row(imap, child, 0, r) == 0) for child in (h, 1 - h)]
+            hit = []
+            for g in range(4):
+                for w, child in enumerate((h, 1 - h)):
+                    lands, lc = place(imap, child, g, h, z, core)
+                    hit.append((w, g, lands & row_in[w], lc))
+            for lc in range(4):
+                weights = [(w, g, jnp.where(ok & (at == lc), 1.0, 0.0).astype(f32)) for w, g, ok, at in hit]
+                present = mask[r, c + 16 * lc].astype(f32)
+
+                @pl.loop(0, 8)
+                def _(q):
+                    rows = pl.ds(pl.multiple_of(q * 32, 32), 32)
+                    total = FR[rows, lc * BS:(lc + 1) * BS]
+                    for w, g, weight in weights:
+                        total = total + weight * (RBr if w == 0 else RBx)[g, rows, :]
+                    PR[rows, lc * BS:(lc + 1) * BS] = total * present
+            send_row_panel()
+
+    def make_row_panel_free():
+        @pl.when(is_row_source)
+        def _():
+            load_fr.wait()
+            for lc in range(4):
+                PR[:, lc * BS:(lc + 1) * BS] = (
+                    FR[:, lc * BS:(lc + 1) * BS] * mask[r, c + 16 * lc].astype(f32)
+                )
+            send_row_panel()
 
     panel = 2 * z + core
 
@@ -231,52 +244,71 @@
     shift = [0, 0, 1, 3, 1, 3, 2, 2]
     own_l = pltpu.make_async_copy(PC, LR.at[jnp.minimum(panel, 3)], lcopy.at[0])
 
-    @pl.when(is_col_source)
-    def _():
-        @pl.when(z == 0)
-        def _():
-            for jj in range(4):
-                if jj > 0:
+    def send_column_block(l, value):
+        PC[l] = value
+        l_copy(z, l, PC.at[l]).start()
+        if shift[l] == 0:
+            l_x_source(l).start()
+
+    def make_column_panel():
+        @pl.when(is_col_source)
+        def _():
+            @pl.when(z == 0)
+            def _():
+                for jj in range(4):
+                    if jj > 0:
+                        x_copy(jj, 0).wait_recv()
+
+            @pl.when(z != 0)
+            def _():
+                for jj in range(1, 4):
                     x_copy(jj, 0).wait_recv()
 
+            @pl.when(r >= 4)
+            def _():
+                x_copy(0, 0).wait_recv()
+
+            from_r = pltpu.make_async_copy(R.at[0], RCr, ldc.at[0])
+            from_x = pltpu.make_async_copy(X.at[0], RCx, ldc.at[1])
+            from_r.start()
+            from_x.start()
+            load_fc.wait()
+            from_r.wait()
+            from_x.wait()
+            hits = [place(imap, child, 0, h, z, core) for child in (h, 1 - h)]
+            rows_at = [[local_row(imap, child, jj, r) for jj in range(4)] for child in (h, 1 - h)]
+            for l in range(8):
+                present = mask[r + 8 * l, c].astype(f32)
+                total = FC[l * BS:(l + 1) * BS, :]
+                for w, source in enumerate((RCr, RCx)):
+                    lands, lc = hits[w]
+                    index = jnp.int32(0)
+                    found = jnp.int32(0)
+                    for jj in range(4):
+                        here = (rows_at[w][jj] == l).astype(jnp.int32)
+                        index = jnp.where(here > 0, jj, index)
+                        found = found + here
+                    weight = jnp.where(lands & (lc == 0) & (found > 0), 1.0, 0.0).astype(f32)
+                    total = total + weight * source[index]
+                send_column_block(l, total * present)
+            own_l.start()
+
+    def make_column_panel_free():
+        @pl.when(is_col_source)
+        def _():
+            load_fc.wait()
+            for l in range(8):
+                send_column_block(l, FC[l * BS:(l + 1) * BS, :] * mask[r + 8 * l, c].astype(f32))
+            own_l.start()
+
+    def group0_early():
         @pl.when(z != 0)
         def _():
             for jj in range(1, 4):
-                x_copy(jj, 0).wait_recv()
-
-        @pl.when(r >= 4)
-        def _():
-            x_copy(0, 0).wait_recv()
-
-        from_r = pltpu.make_async_copy(R.at[0], RCr, ldc.at[0])
-        from_x = pltpu.make_async_copy(X.at[0], RCx, ldc.at[1])
-        from_r.start()
-        from_x.start()
-        load_fc.wait()
-        from_r.wait()
-        from_x.wait()
-        hits = [place(imap, child, 0, h, z, core) for child in (h, 1 - h)]
-        rows_at = [[local_row(imap, child, jj, r) for jj in range(4)] for child in (h, 1 - h)]
-        for l in range(8):
-            present = mask[r + 8 * l, c].astype(f32)
-            total = FC[l * BS:(l + 1) * BS, :]
-            for w, source in enumerate((RCr, RCx)):
-                lands, lc = hits[w]
-                index = jnp.int32(0)
-                found = jnp.int32(0)
-                for jj in range(4):
-                    here = (rows_at[w][jj] == l).astype(jnp.int32)
-                    index = jnp.where(here > 0, jj, index)
-                    found = found + here
-                weight = jnp.where(lands & (lc == 0) & (found > 0), 1.0, 0.0).astype(f32)
-                total = total + weight * source[index]
-            PC[l] = total * present
-            l_copy(z, l, PC.at[l]).start()
-            if shift[l] == 0:
-                l_x_source(l).start()
-        own_l.start()
-
-    for jj in range(1, 4):
+                z_wait(jj, 0)
+                x_copy(jj, 0).start()
+
+    def rest_x(jj):
         for d in (1, 3, 2):
             g = (z + d) % 4
 
@@ -285,47 +317,100 @@
                 z_wait(jj, g)
                 x_copy(jj, g).start()
 
-    @pl.when(is_col_source)
-    def _():
-        own_l.wait()
-
-    def at_source(s):
-        return (h == 0) & (z == s)
-
-    def column_step(s, l):
-        dist = (z + 4 - s) % 4 if l % 2 == 0 else (s + 4 - z) % 4
-        cross_z = (s + shift[l]) % 4
-
-        @pl.when(jnp.logical_not(at_source(s)))
-        def _():
-            l_wait(s, l)
-
+    def own_l_wait():
+        @pl.when(is_col_source)
+        def _():
+            own_l.wait()
+
+    def column_ring(step):
+        for i in range(4):
+            if not 1 <= step - i <= 3:
+                continue
+            for way in range(2):
+                l = 2 * i + way
+                for s in range(2):
+                    dist = (z + 4 - s) % 4 if way == 0 else (s + 4 - z) % 4
+
+                    @pl.when(dist == step - i)
+                    def _():
+                        l_wait(s, l)
+                        if step - i < 3:
+                            l_copy(s, l, LR.at[2 * s + core, l]).start()
+                        if shift[l] != 0:
+                            @pl.when(z == (s + shift[l]) % 4)
+                            def _():
+                                l_x(s, l).start()
+
+                        l_core(s, l).start()
+
+    def column_spread(l):
+        for s in range(2):
+            @pl.when(z == (s + shift[l]) % 4)
+            def _():
+                l_wait(s, l)
+                for d in (1, 3, 2):
+                    l_three(s, l, d).start()
+                l_core(s, l).start()
+
+    def column_rest(l):
+        for s in range(2):
+            @pl.when(z != (s + shift[l]) % 4)
+            def _():
+                l_wait(s, l)
+                l_core(s, l).start()
+
+    def column_slot(slot):
         @pl.when(h == 0)
         def _():
-            @pl.when((dist > 0) & (dist < 3))
-            def _():
-                l_copy(s, l, LR.at[2 * s + core, l]).start()
-
-            if shift[l] != 0:
-                @pl.when(z == cross_z)
-                def _():
-                    l_x(s, l).start()
-
-        @pl.when((h == 1) & (z == cross_z))
-        def _():
-            for d in (1, 3, 2):
-                l_three(s, l, d).start()
-
-        l_core(s, l).start()
-
-    def c_next(s):
-        return y_peer((y + (1 if s == 0 else 3)) % 4)
-
-    def c_copy(k, s, src):
-        return remote(src, CR.at[k, core, s], Cs.at[k, s], Cr.at[k, s], c_next(s))
-
-    def c_partner(s):
-        return remote(LR.at[2 * s + core, 0], CR.at[r, core, s], Cps.at[s], Cr.at[r, s], e_peer)
+            if slot == 1:
+                own_l_wait()
+                for l in range(8):
+                    @pl.when(z < 2)
+                    def _():
+                        l_core(z, l).start()
+
+            column_ring(slot)
+            if slot == 3 and has["C"]:
+                corner_start()
+
+        @pl.when(h == 1)
+        def _():
+            if slot == 1:
+                column_spread(0)
+                column_spread(1)
+            if slot == 2:
+                column_rest(0)
+                if has["C"]:
+                    corner_start()
+            if slot == 3:
+                column_spread(2)
+                column_spread(3)
+                column_rest(1)
+            if slot == 4:
+                column_spread(4)
+                column_spread(5)
+                column_rest(2)
+                column_rest(3)
+            if slot == 5:
+                column_rest(4)
+                column_rest(5)
+            if slot == 6:
+                column_spread(6)
+                column_spread(7)
+                column_rest(6)
+                column_rest(7)
+
+    def c_held(k, s, q):
+        return CR.at[k, core, s, pl.ds(128 * q, 128)]
+
+    def c_from(s, q):
+        return LR.at[2 * s + core, 0, pl.ds(128 * q, 128)]
+
+    def c_copy(k, s, q, src):
+        return remote(src, c_held(k, s, q), Cs.at[k, s, q], Cr.at[k, s, q], y_next(s))
+
+    def c_partner(s, q):
+        return remote(c_from(s, q), c_held(r, s, q), Cps.at[s, q], Cr.at[r, s, q], e_peer)
 
     def c_own(s):
         return pltpu.make_async_copy(
@@ -339,71 +424,111 @@
         s = k // 2
         return (y + 4 - s) % 4 if way == 0 else (s + 4 - y) % 4
 
-    def row_step(k, half):
-        dist = ring_dist(k, half)
-
-        @pl.when(r != k)
-        def _():
-            u_copy(k, half, UR.at[k, pl.ds(half * 128, 128)]).wait_recv()
-
-            @pl.when(dist < 3)
-            def _():
-                u_copy(k, half, UR.at[k, pl.ds(half * 128, 128)]).start()
-
-    def corner_step(k, s):
-        dist = ring_dist(k, s)
-
-        @pl.when(r != k)
-        def _():
-            c_copy(k, s, CR.at[k, core, s]).wait_recv()
-
-            @pl.when(dist < 3)
-            def _():
-                c_copy(k, s, CR.at[k, core, s]).start()
-
-    for s in range(2):
-        column_step(s, 0)
-
-    @pl.when(is_row_source)
-    def _():
-        for s in range(2):
-            c_own(s).start()
-            c_partner(s).start()
-            c_copy(r, s, LR.at[2 * s + core, 0]).start()
-
-    for s in range(2):
-        column_step(s, 1)
-    for k in range(4):
-        for half in range(2):
-            row_step(k, half)
-    for l in (2, 3):
-        for s in range(2):
-            column_step(s, l)
-    for k in range(4):
-        for s in range(2):
-            corner_step(k, s)
-
-        @pl.when(r == k)
+    def row_ring(step):
+        for q in range(2):
+            if not 0 <= step - q <= 3:
+                continue
+            for k in range(4):
+                for way in range(2):
+                    @pl.when((r != k) & (ring_dist(k, way) == step - q))
+                    def _():
+                        u_copy(k, way, q, u_held(k, way, q)).wait_recv()
+                        if step - q < 3:
+                            u_copy(k, way, q, u_held(k, way, q)).start()
+
+    def corner_ring(step):
+        for q in range(2):
+            if not 0 <= step - q <= 3:
+                continue
+            for k in range(4):
+                for s in range(2):
+                    @pl.when((r != k) & (ring_dist(k, s) == step - q))
+                    def _():
+                        c_copy(k, s, q, c_held(k, s, q)).wait_recv()
+                        if step - q < 3:
+                            c_copy(k, s, q, c_held(k, s, q)).start()
+
+    def corner_start():
+        @pl.when(is_row_source)
+        def _():
+            for q in range(2):
+                for s in range(2):
+                    c_partner(s, q).start()
+                    c_copy(r, s, q, c_from(s, q)).start()
+            for s in range(2):
+                c_own(s).start()
+
+    def corner_swap():
+        @pl.when(is_row_source)
         def _():
             for s in range(2):
                 c_own(s).wait()
 
-        c_core(k).start()
-    for l in (4, 5, 6, 7):
-        for s in range(2):
-            column_step(s, l)
-
-    for jj in range(4):
+        for k in range(4):
+            c_core(k).start()
+
+    def slots(free):
+        for slot in range(1, 7):
+            if has["L"]:
+                column_slot(slot)
+            if has["U"] and slot <= 5:
+                row_ring(slot - 1)
+            if has["X"]:
+                if free:
+                    if slot == 2:
+                        own_waits()
+                    if 2 <= slot <= 5:
+                        for d in (1, 3, 2):
+                            forward_x(slot - 2, d)
+                elif slot <= 3:
+                    rest_x(slot)
+            if has["C"]:
+                for step in {4: (0,), 5: (1,), 6: (2, 3, 4)}.get(slot, ()):
+                    corner_ring(step)
+        if has["C"]:
+            corner_swap()
+
+    if free:
+        if has["L"]:
+            make_column_panel_free()
+        if has["U"]:
+            make_row_panel_free()
+        if has["X"]:
+            swap_cores()
+            for jj in range(4):
+                arrange(jj)
+                x_own(jj).start()
+    else:
+        swap_cores()
+        for jj in range(4):
+            arrange(jj)
+            if jj == 0:
+                x_own(jj).start()
+        for d in (1, 3, 2):
+            forward_x(0, d)
+        group0_early()
+        for jj in range(1, 4):
+            x_own(jj).start()
+        own_waits()
+        if has["U"]:
+            make_row_panel()
+        if has["L"]:
+            make_column_panel()
+    slots(free)
+
+    for jj in range(4) if has["X"] else ():
         core_copy(jj).wait_send()
         for d in (1, 2, 3):
             z_copy(jj, d).wait_send()
         for g in range(4):
             x_copy(jj, g).wait_send()
 
-    for g in range(4):
+    for g in range(4) if has["X"] else ():
         for jj in range(4):
-            done = jnp.bool_(False)
-            if jj == 0:
+            done = never
+            if free:
+                pass
+            elif jj == 0:
                 done = is_row_source | ((g == 0) & is_col_source)
             elif g == 0:
                 done = is_col_source
@@ -415,23 +540,27 @@
     @pl.when(is_row_source)
     def _():
         own_u.wait()
-        for half in range(2):
-            u_partner(half).wait_send()
-            u_copy(r, half, PR.at[pl.ds(half * 128, 128)]).wait_send()
-        for s in range(2):
-            c_partner(s).wait_send()
-            c_copy(r, s, LR.at[2 * s + core, 0]).wait_send()
-    for k in range(4):
+        for q in range(2):
+            for way in range(2):
+                u_partner(way, q).wait_send()
+                u_copy(r, way, q, PR.at[u_rows(way, q)]).wait_send()
+                if has["C"]:
+                    c_partner(way, q).wait_send()
+                    c_copy(r, way, q, c_from(way, q)).wait_send()
+    for k in range(4) if has["U"] else ():
         for way in range(2):
             dist = ring_dist(k, way)
 
             @pl.when((r != k) & (dist < 3))
             def _():
-                u_copy(k, way, UR.at[k, pl.ds(way * 128, 128)]).wait_send()
-                c_copy(k, way, CR.at[k, core, way]).wait_send()
-
-        c_core(k).wait()
-    for s in range(2):
+                for q in range(2):
+                    u_copy(k, way, q, u_held(k, way, q)).wait_send()
+                    if has["C"]:
+                        c_copy(k, way, q, c_held(k, way, q)).wait_send()
+
+        if has["C"]:
+            c_core(k).wait()
+    for s in range(2) if has["L"] else ():
         for l in range(8):
             dist = (z + 4 - s) % 4 if l % 2 == 0 else (s + 4 - z) % 4
             cross_z = (s + shift[l]) % 4
@@ -561,7 +690,7 @@
     dma = pltpu.SemaphoreType.DMA
     blk = (BS, BS)
     R, X, LR, UR, CR = pl.pallas_call(
-        exchange_kernel,
+        functools.partial(exchange_kernel, FREE, PARTS),
         out_shape=[
             jax.ShapeDtypeStruct((4, 4) + blk, f32),
             jax.ShapeDtypeStruct((4, 4) + blk, f32),
@@ -581,8 +710,8 @@
             dma((4, 4)), dma((4,)),
             dma((2, 4)), dma((2,)), dma((1,)), dma((2, 8)), dma((2, 8)), dma((2, 8)), dma((2, 8)),
             dma((2, 8)), dma((2, 8, 4)),
-            dma((4, 2)), dma((4, 2)), dma((2,)), dma((1,)), dma((4, 2)), dma((4, 2)), dma((2,)),
-            dma((2,)), dma((4,)), dma((4,)),
+            dma((4, 2, 2)), dma((4, 2, 2)), dma((2, 2)), dma((1,)), dma((4, 2, 2)), dma((4, 2, 2)),
+            dma((2, 2)), dma((2,)), dma((4,)), dma((4,)),
         ],
         compiler_params=pltpu.CompilerParams(
             collective_id=0, has_side_effects=True, vmem_limit_bytes=48 * 2**20

time: 554 us -> 261 us (0.47)
  the two profiles are of different devices: /device:TPU:118 before, /device:TPU:39 now
where the time goes in v2:
time: 261 us
  Pallas kernels  252 us (97%)
  local copies, waits for them, and re-layouts  7.77 us (3%)
    pallas_call x1, Pallas kernels, body(): pl.pallas_call(functools.partial(exchange_kernel, FREE, PARTS), out_shape...  211 us
    pallas_call x1, Pallas kernels, body(): pl.pallas_call(update_kernel, out_shape=jax.ShapeDtypeStruct(front.shape,...  24.7 us
    pallas_call x1, Pallas kernels, body(): pl.pallas_call(panel_kernel, out_shape=[jax.ShapeDtypeStruct((4 * BS, 4 *...  16.8 us
    unnamed x18, local copies, waits for them, and re-layouts  7.77 us

profile of v2, /device:TPU:39, one launch (start us, length us, event | category | flops | bytes accessed | tf_op | source)
XLA Modules:
  0.0 260.6 jit_solution(2863749146492494604)
XLA Ops:
  0.0 0.6 pad_add_fusion.pos
  0.6 0.0 copy-start.4
  0.6 0.8 copy-done.4
  1.3 0.0 copy-start.6
  1.3 0.7 copy-done.6
  2.0 210.7 %exchange.1 = (f32[4,4,256,256]{3,2,1,0:T(8,128)S(1)}, f32[4,4,256,256]{3,2,1,0:T(8,128)}, f32[4,8,256,256]{3,2,1,0:T(8,128)}, f32[4,256,1024]{2,1,0:T(8,128)}, f32[4,2,2,256,256]{4,3,2,1,0:T(8,128)}) custom-call(s32[2,32]{1,0:T(2,128)S(1)} %copy-done.6, s32[64,64]{1,0:T(8,128)S(1)} %copy-done.4, f32[1024,1024]{1,0:T(8,128)} %contrib.1, f32[2048,1024]{1,0:T(8,128)} %F.1), custom_call_target="tpu_custom_call" | custom-call | tf_op jit(solution)/shard_map/exchange/pallas_call | solution.py:692
  212.8 0.0 copy-start
  212.8 1.9 copy-done
  214.7 0.0 copy-start.5
  214.7 0.0 copy-start.7
  214.7 0.0 copy-start.8
  214.7 16.8 %panel.1 = (bf16[1024,1024]{1,0:T(8,128)(2,1)}, bf16[1024,1024]{1,0:T(8,128)(2,1)}, f32[256,1024]{1,0:T(8,128)}) custom-call(s32[2]{0:T(128)} %pad_add_fusion.pos, f32[4,2,2,256,256]{4,3,2,1,0:T(8,128)} %get-tuple-element.16.CR, f32[4,256,1024]{2,1,0:T(8,128)} %get-tuple-element.17.UR, f32[4,256,256]{2,1,0:T(8,128)} %pinv.1), custom_call_target="tpu_custom_call" | custom-call | tf_op jit(solution)/shard_map/panel/pallas_call | solution.py:722
  231.5 0.0 copy-done.5
  231.5 0.0 copy-done.7
  231.5 0.0 copy-done.8
  231.5 0.0 copy-start.1
  231.5 1.6 copy-done.1
  233.1 0.0 copy-start.2
  233.1 1.6 copy-done.2
  234.7 0.0 copy-start.3
  234.7 1.2 copy-done.3
  235.9 24.7 %update.1 = f32[2048,1024]{1,0:T(8,128)} custom-call(s32[2,32]{1,0:T(2,128)S(1)} %copy-done.7, s32[64,64]{1,0:T(8,128)S(1)} %copy-done.5, s32[2]{0:T(128)S(1)} %copy-done.8, f32[2048,1024]{1,0:T(8,128)} %F.1, f32[4,8,256,256]{3,2,1,0:T(8,128)} %get-tuple-element.13.LRl, f32[4,4,256,256]{3,2,1,0:T(8,128)} %copy-done, f32[4,4,256,256]{3,2,1,0:T(8,128)} %get-tuple-element.15.X, ...), custom_call_target="tpu_custom_call" | custom-call | tf_op jit(solution)/shard_map/update/pallas_call | solution.py:745
Async XLA Ops:
  0.6 0.8 copy-start.4
  1.3 0.7 copy-start.6
  212.8 1.9 copy-start
  214.7 16.8 %copy-start.5 = (s32[64,64]{1,0:T(8,128)S(1)}, s32[64,64]{1,0:T(8,128)}, u32[]{:S(2)}) copy-start(s32[64,64]{1,0:T(8,128)} %mask.3) | copy-start | bytes 49156
  214.7 16.8 %copy-start.7 = (s32[2,32]{1,0:T(2,128)S(1)}, s32[2,32]{1,0:T(2,128)}, u32[]{:S(2)}) copy-start(s32[2,32]{1,0:T(2,128)} %imap.3) | copy-start | bytes 772
  214.7 16.8 %copy-start.8 = (s32[2]{0:T(128)S(1)}, s32[2]{0:T(128)}, u32[]{:S(2)}) copy-start(s32[2]{0:T(128)} %pad_add_fusion.pos) | copy-start | bytes 28
  231.5 1.6 copy-start.1
  233.1 1.6 copy-start.2
  234.7 1.2 copy-start.3
